TPU v7x, 512 devices: a whole 4x4x16 slice. The times are simulated.
512 devices in a mesh: dp: 32 (over z, core), mp: 16 (over y, x).
Axes of the slice: x: 4, y: 4, z: 16, core: 2. Of those that a mesh axis runs over, the one named last changes fastest.
Arguments:
- grad: bfloat16 [32, 512, 6144], P(None, 'dp', 'mp'), may hold values from -100 to 100
- momentum: float32 [32, 512, 6144], P(None, 'dp', 'mp'), may hold values from -200 to 200
- old_slot: int32 [32], replicated, may hold values from 0 to 31, each once
- new_slot: int32 [32], replicated, may hold values from 0 to 31, each once
Outputs:
- new_momentum: float32 [32, 512, 6144], P(None, 'dp', 'mp')
- update: bfloat16 [32, 512, 6144], P(None, 'dp', 'mp')
Inputs may be any that keep to these rules, and one draw needn't show every extreme that they name: old_slot and new_slot are each a permutation of the matrices. `new_slot`: a permutation.
All inputs are finite; a program needn't handle non-finite values.
Results may differ from a plain program's by a relative error of at most 0.0053.
Values may be sent and summed in bfloat16 or wider, within the bound.
No kernel may reach another device: no remote copies, remote signals or barrier semaphores. Data moves between devices by JAX's collectives and lax.ppermute only.
A program may use at most 64 MiB of HBM per device.

v0:
```python
import math

import jax
import jax.numpy as jnp
from jax import lax
from jax.sharding import PartitionSpec as P

ITERS = 3


coef_a = 3.4445
coef_b = -4.775
coef_c = 2.0315
beta = 0.95
epsilon = 1e-07
highest = lax.Precision.HIGHEST


def inverse_of(order):
    count = order.shape[0]
    column = jnp.arange(count, dtype=jnp.int32)
    marks = order[None, :] == column[:, None]
    return jnp.sum(jnp.where(marks, column[None, :], 0), axis=1)


def polish(start):
    start_wide = start.astype(jnp.float32)
    total = lax.psum(jnp.sum(start_wide * start_wide), "mp")
    current = start_wide / (jnp.sqrt(total) + epsilon)
    width = start.shape[1] * lax.axis_size("mp")
    for step in range(ITERS):
        partial_value = lax.dot_general(
            current,
            current,
            (((1,), (1,)), ((), ())),
            precision=highest,
            preferred_element_type=jnp.float32,
        )
        gram = lax.psum(partial_value, "mp")
        square = jnp.dot(gram, gram, precision=highest, preferred_element_type=jnp.float32)
        poly = coef_b * gram + coef_c * square
        current = coef_a * current + jnp.dot(
            poly, current, precision=highest, preferred_element_type=jnp.float32
        )
    return (0.2 * math.sqrt(width) * current).astype(jnp.bfloat16)


def body(grad, momentum, old_slot, new_slot):
    grad_by = jnp.take(grad, new_slot, axis=0)
    mom_by = jnp.take(momentum, old_slot, axis=0)
    placing = inverse_of(new_slot)
    merged = beta * mom_by + grad_by.astype(jnp.float32)
    got = lax.all_to_all(merged.astype(jnp.bfloat16), "dp", split_axis=0, concat_axis=1, tiled=True)
    update = polish(got[0])[None]
    back_upd = lax.all_to_all(update, "dp", split_axis=1, concat_axis=0, tiled=True)
    return (jnp.take(merged, placing, axis=0), jnp.take(back_upd, placing, axis=0))


def solution(mesh):
    placed = (P(None, "dp", "mp"), P(None, "dp", "mp"), P(), P())
    return jax.shard_map(
        body,
        mesh=mesh,
        in_specs=placed,
        out_specs=(P(None, "dp", "mp"), P(None, "dp", "mp")),
        check_vma=False,
    )
```

profile of v0, /device:TPU:1, one launch (start us, length us, event | category | flops | bytes accessed | tf_op | source)
XLA Modules:
  0.0 516.6 jit_solution(11566304208362995942)
XLA Ops:
  7.2 0.7 compare_select_fusion.2
  8.0 0.3 copy-done
  8.4 0.6 gather_fusion
  9.0 0.4 copy-done.1
  9.3 0.6 gather_fusion.1
  10.0 0.2 fusion.8
  10.2 44.5 %all_to_all.21 = bf16[32,16,384]{2,1,0:T(8,128)(2,1)S(1)} all-to-all(bf16[32,16,384]{2,1,0:T(8,128)(2,1)S(1)} %get-tuple-element.4), channel_id=1, replica_groups=mesh['dp'=32,'mp'=16] {'dp'}, dimensions={0} | all-to-all | bytes 786432 | tf_op jit(solution)/shard_map/all_to_all | solution.py:53
  54.8 0.8 fusion.6
  55.6 34.0 %psum.28 = f32[]{:T(128)} all-reduce(f32[]{:T(128)} %fusion.6), channel_id=1, replica_groups=mesh['dp'=32,'mp'=16] {'mp'}, use_global_device_ids=true, to_apply=%region_2.5 | all-reduce | flops 1 | bytes 8 | tf_op jit(solution)/shard_map/psum | solution.py:28
  90.4 2.9 fusion.10
  93.3 109.8 %all-reduce.4.cloned.1.call-done = f32[512,512]{1,0:T(8,128)} async-done(((f32[512,512]{1,0:T(8,128)}), f32[512,512]{1,0:T(8,128)}) %all-reduce.4.cloned.1.call-update) | async-done | bytes 1048592 | tf_op jit(solution)/shard_map/psum | solution.py:39
  203.1 3.9 fusion.2
  207.0 1.8 convolution_add_fusion.2
  208.9 2.9 fusion.11
  212.0 117.0 %all-reduce.6.cloned.1.call-done = f32[512,512]{1,0:T(8,128)} async-done(((f32[512,512]{1,0:T(8,128)}), f32[512,512]{1,0:T(8,128)}) %all-reduce.6.cloned.1.call-update) | async-done | bytes 1048592 | tf_op jit(solution)/shard_map/psum | solution.py:39
  329.0 3.9 fusion.1
  333.0 1.8 convolution_add_fusion.1
  334.8 2.9 fusion.12
  337.7 117.3 %all-reduce.8.cloned.1.call-done = f32[512,512]{1,0:T(8,128)} async-done(((f32[512,512]{1,0:T(8,128)}), f32[512,512]{1,0:T(8,128)}) %all-reduce.8.cloned.1.call-update) | async-done | bytes 1048592 | tf_op jit(solution)/shard_map/psum | solution.py:39
  454.9 3.9 fusion
  458.9 1.8 fusion.5
  460.7 0.6 copy.11
  461.3 0.5 broadcast.47
  461.8 3.0 reduce.3
  464.8 0.8 reshape.76
  465.7 14.5 %all-to-all-start.1 = ((bf16[32,2,3072]{2,1,0:T(2,128)(2,1)}), bf16[32,2,3072]{2,1,0:T(2,128)(2,1)S(1)}, u32[]{:S(2)}, u32[]{:S(2)}) async-start(bf16[32,2,3072]{2,1,0:T(2,128)(2,1)} %reshape.76), calls=%async_computation.1 | async-start | bytes 786432 | tf_op jit(solution)/shard_map/all_to_all | solution.py:55
  480.4 0.6 gather_fusion.2
  481.0 1.0 broadcast_select_fusion
  482.0 26.2 %all-to-all-done.1 = bf16[32,2,3072]{2,1,0:T(2,128)(2,1)S(1)} async-done(((bf16[32,2,3072]{2,1,0:T(2,128)(2,1)}), bf16[32,2,3072]{2,1,0:T(2,128)(2,1)S(1)}, u32[]{:S(2)}, u32[]{:S(2)}) %all-to-all-start.1) | async-done | bytes 393248 | tf_op jit(solution)/shard_map/all_to_all | solution.py:55
  508.2 0.3 reshape.77
  508.6 0.6 gather_fusion.3
  509.2 0.9 broadcast_select_fusion.1
  (22 shorter events, 0.6 us)
Async XLA Ops:
  7.2 1.2 copy-start
  7.2 0.8 copy-start.2
  7.2 0.8 copy-start.3
  7.2 195.9 %all-reduce.4.cloned.1.call-start = ((), (), s32[]{:S(2)}) async-start(), calls=%async_computation.2 | async-start | bytes 2097152 | tf_op jit(solution)/shard_map/psum | solution.py:39
  8.4 1.0 copy-start.1
  93.3 235.8 %all-reduce.6.cloned.1.call-start = ((), (), s32[]{:S(2)}) async-start(), calls=%async_computation.3 | async-start | bytes 2097152 | tf_op jit(solution)/shard_map/psum | solution.py:39
  211.8 243.2 %all-reduce.8.cloned.1.call-start = ((), (), s32[]{:S(2)}) async-start(), calls=%async_computation.4 | async-start | bytes 2097152 | tf_op jit(solution)/shard_map/psum | solution.py:39
  465.7 42.5 %all-to-all-start.1 = ((bf16[32,2,3072]{2,1,0:T(2,128)(2,1)}), bf16[32,2,3072]{2,1,0:T(2,128)(2,1)S(1)}, u32[]{:S(2)}, u32[]{:S(2)}) async-start(bf16[32,2,3072]{2,1,0:T(2,128)(2,1)} %reshape.76), calls=%async_computation.1 | async-start | bytes 786432 | tf_op jit(solution)/shard_map/all_to_all | solution.py:55
Sparse Core Ops, SparseCore 0:
  93.4 109.6 all-reduce.3
  211.9 117.1 all-reduce.5
  337.8 117.1 all-reduce.7
where the time goes:
time: 517 us
  waiting for transfers between devices  370 us (72%)
  blocking collectives  78.6 us (15%)
  matrix products  25.8 us (5%)
  starting transfers between devices  14.8 us (3%)
  between operations  14.6 us (3%)
  other arithmetic  6.86 us (1%)
  local copies, waits for them, and re-layouts  5.54 us (1%)
    psum x3, waiting for transfers between devices, polish(): gram = lax.psum(partial_value, 'mp')  344 us
    all_to_all x1, blocking collectives, body(): lax.all_to_all(merged.astype(jnp.bfloat16), 'dp', split_axis=0, concat_ax...  44.5 us
    psum x1, blocking collectives, polish(): total = lax.psum(jnp.sum(start_wide * start_wide), 'mp')  34 us
    all_to_all x1, waiting for transfers between devices, body(): lax.all_to_all(update, 'dp', split_axis=1, concat_axis=0, tiled=True)  26.2 us
    all_to_all x1, starting transfers between devices, body(): lax.all_to_all(update, 'dp', split_axis=1, concat_axis=0, tiled=True)  14.5 us
    dot_general x3, matrix products, polish(): jnp.dot(gram, gram, precision=highest, preferred_element_type=jnp.float32)  11.7 us
  transfers between devices with their start and end apart: 4, of which 4 were waited for; matrix products, arithmetic and copies ran while one was open for 0% of the time, Pallas kernels for 0%

commit v1 on v0

v1 whole, which is shorter than its diff:
```python
import math

import jax
import jax.numpy as jnp
from jax import lax
from jax.experimental import pallas as pl
from jax.experimental.pallas import tpu as pltpu
from jax.sharding import PartitionSpec as P

coef_a = 3.4445
coef_b = -4.775
coef_c = 2.0315
beta = 0.95
epsilon = 1e-07
TILE = 128
bf16 = jnp.bfloat16
f32 = jnp.float32


def merge_kernel(
    old_ref, new_ref, grad_ref, mom_ref, merged_ref, start_ref, old, new, grad, mom, merged, sems, done
):
    loads = [
        pltpu.make_async_copy(source, target, sems.at[at])
        for at, (source, target) in enumerate(
            [(mom_ref, mom), (grad_ref, grad), (old_ref, old), (new_ref, new)]
        )
    ]
    for load in loads:
        load.start()
    for load in loads:
        load.wait()
    for j in range(grad.shape[0]):
        slot = new[j]
        value = beta * mom[old[j]] + grad[slot].astype(f32)
        start_ref[slot] = value.astype(bf16)
        merged[slot] = value
    store = pltpu.make_async_copy(merged, merged_ref, done)
    store.start()
    store.wait()


def merge(grad, momentum, old_slot, new_slot):
    hbm = pl.BlockSpec(memory_space=pltpu.HBM)
    return pl.pallas_call(
        merge_kernel,
        out_shape=(
            jax.ShapeDtypeStruct(momentum.shape, f32),
            jax.ShapeDtypeStruct(grad.shape, bf16),
        ),
        in_specs=[hbm] * 4,
        out_specs=(hbm, pl.BlockSpec(memory_space=pltpu.VMEM)),
        scratch_shapes=[
            pltpu.SMEM(old_slot.shape, jnp.int32),
            pltpu.SMEM(new_slot.shape, jnp.int32),
            pltpu.VMEM(grad.shape, bf16),
            pltpu.VMEM(momentum.shape, f32),
            pltpu.VMEM(momentum.shape, f32),
            pltpu.SemaphoreType.DMA((4,)),
            pltpu.SemaphoreType.DMA,
        ],
        compiler_params=pltpu.CompilerParams(vmem_limit_bytes=63 << 20),
    )(old_slot, new_slot, grad, momentum)


def upper(count):
    return [(r, s) for r in range(count) for s in range(r, count)]


def gram_kernel(x_ref, out_ref):
    x = x_ref[...]
    gram = lax.dot_general(x, x, (((1,), (1,)), ((), ())), preferred_element_type=f32)
    for at, (r, s) in enumerate(upper(x.shape[0] // TILE)):
        block = gram[r * TILE : (r + 1) * TILE, s * TILE : (s + 1) * TILE]
        out_ref[at * TILE : (at + 1) * TILE, :] = block


def sum_kernel(parts_ref, out_ref):
    total = parts_ref[0]
    for k in range(1, parts_ref.shape[0]):
        total += parts_ref[k]
    for k in range(parts_ref.shape[0]):
        out_ref[k] = total


def split(value):
    high = value.astype(bf16)
    return high, (value - high.astype(f32)).astype(bf16)


def dot(left, right):
    return jnp.dot(left, right, preferred_element_type=f32)


def product(left, right):
    (lh, ll), (rh, rl) = left, right
    return dot(jnp.concatenate([lh, ll, lh], axis=1), jnp.concatenate([rh, rh, rl], axis=0))


def symmetric(left, right):
    half = left[0].shape[0] // 2
    top = product([p[:half] for p in left], right)
    corner = product([p[half:] for p in left], [p[:, half:] for p in right])
    return jnp.concatenate([top, jnp.concatenate([top[:, half:].T, corner], axis=1)], axis=0)


def polish_kernel(width, packed_ref, x_ref, out_ref, gram_ref):
    rows = x_ref.shape[0]
    for at, (r, s) in enumerate(upper(rows // TILE)):
        block = packed_ref[at * TILE : (at + 1) * TILE, :]
        gram_ref[r * TILE : (r + 1) * TILE, s * TILE : (s + 1) * TILE] = block
        if r != s:
            gram_ref[s * TILE : (s + 1) * TILE, r * TILE : (r + 1) * TILE] = block.T
    gram = gram_ref[...]
    row = lax.broadcasted_iota(jnp.int32, (rows, rows), 0)
    column = lax.broadcasted_iota(jnp.int32, (rows, rows), 1)
    diagonal = row == column
    total = jnp.sum(jnp.where(diagonal, gram, 0.0))
    inverse = 1.0 / (jnp.sqrt(jnp.full((1, 1), total)) + epsilon)
    gram = gram * inverse * inverse
    rests, steps = [], []
    for step in range(3):
        g = split(gram)
        rest = coef_b * gram + coef_c * symmetric(g, g)
        q = split(rest)
        rests.append(rest)
        steps.append(q)
        if step < 2:
            half = coef_a * gram + symmetric(g, q)
        if step == 1:
            both = coef_a * (rests[0] + rests[1]) + symmetric(q, steps[0])
            both += jnp.where(diagonal, coef_a * coef_a, 0.0)
        if step < 2:
            gram = coef_a * half + symmetric(split(half), q)
    whole = split(coef_a * both + symmetric(steps[2], split(both)))
    x = x_ref[...]
    current = dot(whole[0], x) + dot(whole[1], x)
    out_ref[...] = (0.2 * math.sqrt(width) * inverse * current).astype(bf16)


def keep_kernel(in_ref, out_ref, done):
    copy = pltpu.make_async_copy(in_ref, out_ref, done)
    copy.start()
    copy.wait()


def keep(value):
    return pl.pallas_call(
        keep_kernel,
        out_shape=jax.ShapeDtypeStruct(value.shape, value.dtype),
        in_specs=[pl.BlockSpec(memory_space=pl.ANY)],
        out_specs=pl.BlockSpec(memory_space=pltpu.HBM),
        scratch_shapes=[pltpu.SemaphoreType.DMA],
        compiler_params=pltpu.CompilerParams(vmem_limit_bytes=16 << 20),
    )(value)


def polish(start, parts):
    rows, columns = start.shape
    vmem = pl.BlockSpec(memory_space=pltpu.VMEM)
    params = pltpu.CompilerParams(vmem_limit_bytes=48 << 20)
    blocks = len(upper(rows // TILE))
    packed = pl.pallas_call(
        gram_kernel,
        out_shape=jax.ShapeDtypeStruct((blocks * TILE, TILE), f32),
        in_specs=[vmem],
        out_specs=vmem,
        compiler_params=params,
    )(start)
    shares = packed.reshape(parts, blocks * TILE // parts, TILE)
    shares = lax.all_to_all(shares, "mp", split_axis=0, concat_axis=0, tiled=True)
    copies = pl.pallas_call(
        sum_kernel,
        out_shape=jax.ShapeDtypeStruct(shares.shape, f32),
        in_specs=[vmem],
        out_specs=vmem,
        compiler_params=params,
    )(shares)
    copies = lax.all_to_all(copies, "mp", split_axis=0, concat_axis=0, tiled=True)
    return pl.pallas_call(
        lambda *refs: polish_kernel(columns * parts, *refs),
        out_shape=jax.ShapeDtypeStruct(start.shape, bf16),
        in_specs=[vmem, vmem],
        out_specs=vmem,
        scratch_shapes=[pltpu.VMEM((rows, rows), f32)],
        compiler_params=params,
    )(copies.reshape(blocks * TILE, TILE), start)


def body(grad, momentum, old_slot, new_slot):
    merged, start = merge(grad, momentum, old_slot, new_slot)
    got = lax.all_to_all(start, "dp", split_axis=0, concat_axis=0, tiled=True)
    slots, rows, columns = got.shape
    update = polish(got.reshape(slots * rows, columns), lax.axis_size("mp"))
    update = update.reshape(slots, rows, columns)
    return merged, keep(lax.all_to_all(update, "dp", split_axis=0, concat_axis=0, tiled=True))


def solution(mesh):
    placed = (P(None, "dp", "mp"), P(None, "dp", "mp"), P(), P())
    return jax.shard_map(
        body,
        mesh=mesh,
        in_specs=placed,
        out_specs=(P(None, "dp", "mp"), P(None, "dp", "mp")),
        check_vma=False,
    )
```

time: 517 us -> 124 us (0.24)
  waiting for transfers between devices: 370 us -> 0 us
  blocking collectives: 78.6 us -> 111 us
  matrix products: 25.8 us -> 0 us
  starting transfers between devices: 14.8 us -> 0 us
  between operations: 14.6 us -> 0.66 us
  Pallas kernels: 0 us -> 11.6 us
  other arithmetic: 6.86 us -> 0 us
  local copies, waits for them, and re-layouts: 5.54 us -> 0 us
    psum x3 -> x0, waiting for transfers between devices: 344 us -> none  [polish(): gram = lax.psum(partial_value, 'mp')]
    all_to_all x1 -> x4, blocking collectives: 44.5 us -> 111 us  [the longest x1 44.7 us: body(): got = lax.all_to_all(start, 'dp', split_axis=0, concat_axis=0, tiled=True)]
    psum x1 -> x0, blocking collectives: 34 us -> none  [polish(): total = lax.psum(jnp.sum(start_wide * start_wide), 'mp')]
    all_to_all x1 -> x0, waiting for transfers between devices: 26.2 us -> none  [body(): lax.all_to_all(update, 'dp', split_axis=1, concat_axis=0, tiled=True)]
    dot_general x9 -> x0, matrix products: 25.8 us -> none  [the longest x3 11.7 us: polish(): jnp.dot(gram, gram, precision=highest, preferred_element_type=jnp.float32)]
    all_to_all x1 -> x0, starting transfers between devices: 14.5 us -> none  [body(): lax.all_to_all(update, 'dp', split_axis=1, concat_axis=0, tiled=True)]
    pallas_call x0 -> x5, Pallas kernels: none -> 11.6 us  [the longest x1 7.3 us: polish(): pl.pallas_call(lambda *refs: polish_kernel(columns * parts, *refs), out_s...]
  transfers between devices with their start and end apart: 4 -> 0, of which waited for: 4 -> 0; matrix products, arithmetic and copies ran while one was open for 0% -> 0% of each run, Pallas kernels for 0% -> 0%
where the time goes in v1:
time: 124 us
  blocking collectives  111 us (90%)
  Pallas kernels  11.6 us (9%)
    all_to_all x1, blocking collectives, body(): got = lax.all_to_all(start, 'dp', split_axis=0, concat_axis=0, tiled=True)  44.7 us
    all_to_all x1, blocking collectives, body(): lax.all_to_all(update, 'dp', split_axis=0, concat_axis=0, tiled=True)  33.1 us
    all_to_all x1, blocking collectives, polish(): lax.all_to_all(shares, 'mp', split_axis=0, concat_axis=0, tiled=True)  18.5 us
    all_to_all x1, blocking collectives, polish(): lax.all_to_all(copies, 'mp', split_axis=0, concat_axis=0, tiled=True)  15 us
    pallas_call x1, Pallas kernels, polish(): pl.pallas_call(lambda *refs: polish_kernel(columns * parts, *refs), out_s...  7.3 us
    pallas_call x1, Pallas kernels, merge(): pl.pallas_call(merge_kernel, out_shape=(jax.ShapeDtypeStruct(momentum.sha...  3.05 us

profile of v1, /device:TPU:1, one launch (start us, length us, event | category | flops | bytes accessed | tf_op | source)
XLA Modules:
  0.0 123.7 jit_solution(15696825002377849034)
XLA Ops:
  0.6 3.1 %shard_map.59 = (f32[32,16,384]{2,1,0:T(8,128)}, bf16[32,16,384]{2,1,0:T(8,128)(2,1)}) custom-call(s32[32]{0:T(128)} %old_ref.1, s32[32]{0:T(128)} %new_ref.1, bf16[32,16,384]{2,1,0:T(8,128)(2,1)} %grad_ref.1, f32[32,16,384]{2,1,0:T(8,128)} %mom_ref.1), custom_call_target="tpu_custom_call" | custom-call | tf_op jit(solution)/shard_map/pallas_call | solution.py:45
  3.7 44.7 %all_to_all.20 = bf16[32,16,384]{2,1,0:T(8,128)(2,1)S(1)} all-to-all(bf16[32,16,384]{2,1,0:T(8,128)(2,1)} %get-tuple-element.5), channel_id=1, replica_groups=mesh['dp'=32,'mp'=16] {'dp'}, dimensions={0} | all-to-all | bytes 786432 | tf_op jit(solution)/shard_map/all_to_all | solution.py:192
  48.4 0.5 shard_map.60
  48.9 18.5 %all_to_all.21.parts_ref = f32[16,80,128]{2,1,0:T(8,128)S(1)} all-to-all(f32[16,80,128]{2,1,0:T(8,128)S(1)} %bitcast.7), channel_id=1, replica_groups=mesh['dp'=32,'mp'=16] {'mp'}, dimensions={0} | all-to-all | bytes 1310720 | tf_op jit(solution)/shard_map/all_to_all | solution.py:171
  67.4 0.1 shard_map.61
  67.5 15.0 %all_to_all.22 = f32[16,80,128]{2,1,0:T(8,128)S(1)} all-to-all(f32[16,80,128]{2,1,0:T(8,128)S(1)} %shard_map.61), channel_id=1, replica_groups=mesh['dp'=32,'mp'=16] {'mp'}, dimensions={0} | all-to-all | bytes 1310720 | tf_op jit(solution)/shard_map/all_to_all | solution.py:179
  82.5 7.3 %shard_map.62 = bf16[512,384]{1,0:T(8,128)(2,1)S(1)} custom-call(f32[1280,128]{1,0:T(8,128)S(1)} %bitcast.6, bf16[512,384]{1,0:T(8,128)(2,1)S(1)} %bitcast.5), custom_call_target="tpu_custom_call" | custom-call | tf_op jit(solution)/shard_map/pallas_call | solution.py:180
  89.8 33.1 %all_to_all.23.in_ref = bf16[32,16,384]{2,1,0:T(8,128)(2,1)S(1)} all-to-all(bf16[32,16,384]{2,1,0:T(8,128)(2,1)S(1)} %bitcast.8), channel_id=1, replica_groups=mesh['dp'=32,'mp'=16] {'dp'}, dimensions={0} | all-to-all | bytes 786432 | tf_op jit(solution)/shard_map/all_to_all | solution.py:196
  122.9 0.8 shard_map.63

commit v2 on v1

--- a/solution.py
+++ b/solution.py
@@ -18,7 +18,7 @@
 
 
 def merge_kernel(
-    old_ref, new_ref, grad_ref, mom_ref, merged_ref, start_ref, old, new, grad, mom, merged, sems, done
+    old_ref, new_ref, grad_ref, mom_ref, merged_ref, start_ref, old, new, grad, mom, sems
 ):
     loads = [
         pltpu.make_async_copy(source, target, sems.at[at])
@@ -34,10 +34,7 @@
         slot = new[j]
         value = beta * mom[old[j]] + grad[slot].astype(f32)
         start_ref[slot] = value.astype(bf16)
-        merged[slot] = value
-    store = pltpu.make_async_copy(merged, merged_ref, done)
-    store.start()
-    store.wait()
+        merged_ref[slot] = value
 
 
 def merge(grad, momentum, old_slot, new_slot):
@@ -49,38 +46,60 @@
             jax.ShapeDtypeStruct(grad.shape, bf16),
         ),
         in_specs=[hbm] * 4,
-        out_specs=(hbm, pl.BlockSpec(memory_space=pltpu.VMEM)),
+        out_specs=(pl.BlockSpec(memory_space=pltpu.VMEM),) * 2,
         scratch_shapes=[
             pltpu.SMEM(old_slot.shape, jnp.int32),
             pltpu.SMEM(new_slot.shape, jnp.int32),
             pltpu.VMEM(grad.shape, bf16),
             pltpu.VMEM(momentum.shape, f32),
-            pltpu.VMEM(momentum.shape, f32),
             pltpu.SemaphoreType.DMA((4,)),
-            pltpu.SemaphoreType.DMA,
         ],
-        compiler_params=pltpu.CompilerParams(vmem_limit_bytes=63 << 20),
-    )(old_slot, new_slot, grad, momentum)
+        compiler_params=pltpu.CompilerParams(vmem_limit_bytes=32 << 20),
+    )(*(pltpu.with_memory_space_constraint(x, pltpu.HBM) for x in (old_slot, new_slot, grad, momentum)))
 
 
 def upper(count):
     return [(r, s) for r in range(count) for s in range(r, count)]
+
+
+def exponent(bound):
+    return jnp.floor(jnp.log(jnp.maximum(bound, 1e-30)) * (1.0 / math.log(2.0))) - 14.0
+
+
+def power(value):
+    return jnp.exp(value * math.log(2.0))
+
+
+def spot(rows):
+    row = lax.broadcasted_iota(jnp.int32, (rows, TILE), 0)
+    return (row % 8 == 7) & (lax.broadcasted_iota(jnp.int32, (rows, TILE), 1) == 0)
 
 
 def gram_kernel(x_ref, out_ref):
     x = x_ref[...]
     gram = lax.dot_general(x, x, (((1,), (1,)), ((), ())), preferred_element_type=f32)
+    wide = x.astype(f32)
+    bound = jnp.max(jnp.sum(wide * wide, axis=1, keepdims=True), axis=0, keepdims=True)
+    power_of = exponent(bound)
+    gram = gram * power(-power_of)
+    parts = out_ref.shape[0]
     for at, (r, s) in enumerate(upper(x.shape[0] // TILE)):
         block = gram[r * TILE : (r + 1) * TILE, s * TILE : (s + 1) * TILE]
-        out_ref[at * TILE : (at + 1) * TILE, :] = block
+        if at == 0:
+            block = jnp.where(spot(TILE), power_of, block)
+        out_ref[:, at * 8 : (at + 1) * 8, :] = block.reshape(parts, 8, TILE)
 
 
 def sum_kernel(parts_ref, out_ref):
-    total = parts_ref[0]
-    for k in range(1, parts_ref.shape[0]):
-        total += parts_ref[k]
+    total = jnp.zeros(out_ref.shape, f32)
     for k in range(parts_ref.shape[0]):
-        out_ref[k] = total
+        total += parts_ref[k] * power(parts_ref[k, 7:8, 0:1])
+    row = lax.broadcasted_iota(jnp.int32, out_ref.shape, 0)
+    marks = (row == 7) & (lax.broadcasted_iota(jnp.int32, out_ref.shape, 1) == 0)
+    total = jnp.where(marks, 0.0, total)
+    bound = jnp.max(jnp.max(jnp.abs(total), axis=1, keepdims=True), axis=0, keepdims=True)
+    power_of = exponent(bound)
+    out_ref[...] = jnp.where(marks, power_of, total * power(-power_of))
 
 
 def split(value):
@@ -104,10 +123,18 @@
     return jnp.concatenate([top, jnp.concatenate([top[:, half:].T, corner], axis=1)], axis=0)
 
 
-def polish_kernel(width, packed_ref, x_ref, out_ref, gram_ref):
+def polish_kernel(width, packed_ref, x_ref, merged_ref, out_ref, kept_ref, gram_ref, done):
+    store = pltpu.make_async_copy(merged_ref, kept_ref, done)
+    store.start()
     rows = x_ref.shape[0]
+    parts = packed_ref.shape[0]
+    scale = power(packed_ref[:, 7:8, 0:1])
+    row = lax.broadcasted_iota(jnp.int32, (TILE, TILE), 0)
+    below = row > lax.broadcasted_iota(jnp.int32, (TILE, TILE), 1)
     for at, (r, s) in enumerate(upper(rows // TILE)):
-        block = packed_ref[at * TILE : (at + 1) * TILE, :]
+        block = (packed_ref[:, at * 8 : (at + 1) * 8, :] * scale).reshape(TILE, TILE)
+        if r == s:
+            block = jnp.where(below, block.T, block)
         gram_ref[r * TILE : (r + 1) * TILE, s * TILE : (s + 1) * TILE] = block
         if r != s:
             gram_ref[s * TILE : (s + 1) * TILE, r * TILE : (r + 1) * TILE] = block.T
@@ -136,6 +163,7 @@
     x = x_ref[...]
     current = dot(whole[0], x) + dot(whole[1], x)
     out_ref[...] = (0.2 * math.sqrt(width) * inverse * current).astype(bf16)
+    store.wait()
 
 
 def keep_kernel(in_ref, out_ref, done):
@@ -155,43 +183,47 @@
     )(value)
 
 
-def polish(start, parts):
+def polish(start, merged, parts):
     rows, columns = start.shape
     vmem = pl.BlockSpec(memory_space=pltpu.VMEM)
     params = pltpu.CompilerParams(vmem_limit_bytes=48 << 20)
-    blocks = len(upper(rows // TILE))
+    share = (len(upper(rows // TILE)) * 8, TILE)
     packed = pl.pallas_call(
         gram_kernel,
-        out_shape=jax.ShapeDtypeStruct((blocks * TILE, TILE), f32),
+        out_shape=jax.ShapeDtypeStruct((parts, *share), f32),
         in_specs=[vmem],
         out_specs=vmem,
         compiler_params=params,
     )(start)
-    shares = packed.reshape(parts, blocks * TILE // parts, TILE)
-    shares = lax.all_to_all(shares, "mp", split_axis=0, concat_axis=0, tiled=True)
-    copies = pl.pallas_call(
+    packed = packed.astype(jnp.float16)
+    packed = lax.all_to_all(packed, "mp", split_axis=0, concat_axis=0, tiled=True)
+    total = pl.pallas_call(
         sum_kernel,
-        out_shape=jax.ShapeDtypeStruct(shares.shape, f32),
+        out_shape=jax.ShapeDtypeStruct(share, f32),
         in_specs=[vmem],
         out_specs=vmem,
         compiler_params=params,
-    )(shares)
+    )(packed.astype(f32))
+    copies = jnp.broadcast_to(total.astype(jnp.float16), (parts, *share))
     copies = lax.all_to_all(copies, "mp", split_axis=0, concat_axis=0, tiled=True)
     return pl.pallas_call(
         lambda *refs: polish_kernel(columns * parts, *refs),
-        out_shape=jax.ShapeDtypeStruct(start.shape, bf16),
-        in_specs=[vmem, vmem],
-        out_specs=vmem,
-        scratch_shapes=[pltpu.VMEM((rows, rows), f32)],
+        out_shape=(
+            jax.ShapeDtypeStruct(start.shape, bf16),
+            jax.ShapeDtypeStruct(merged.shape, f32),
+        ),
+        in_specs=[vmem] * 3,
+        out_specs=(vmem, pl.BlockSpec(memory_space=pltpu.HBM)),
+        scratch_shapes=[pltpu.VMEM((rows, rows), f32), pltpu.SemaphoreType.DMA],
         compiler_params=params,
-    )(copies.reshape(blocks * TILE, TILE), start)
+    )(copies.astype(f32), start, merged)
 
 
 def body(grad, momentum, old_slot, new_slot):
     merged, start = merge(grad, momentum, old_slot, new_slot)
     got = lax.all_to_all(start, "dp", split_axis=0, concat_axis=0, tiled=True)
     slots, rows, columns = got.shape
-    update = polish(got.reshape(slots * rows, columns), lax.axis_size("mp"))
+    update, merged = polish(got.reshape(slots * rows, columns), merged, lax.axis_size("mp"))
     update = update.reshape(slots, rows, columns)
     return merged, keep(lax.all_to_all(update, "dp", split_axis=0, concat_axis=0, tiled=True))
 

time: 124 us -> 115 us (0.927)
  blocking collectives: 111 us -> 104 us
  Pallas kernels: 11.6 us -> 10.2 us
    all_to_all x1, blocking collectives: 15 us -> 10.7 us  [polish(): lax.all_to_all(copies, 'mp', split_axis=0, concat_axis=0, tiled=True)]
    all_to_all x1, blocking collectives: 18.5 us -> 15.2 us  [polish(): lax.all_to_all(packed, 'mp', split_axis=0, concat_axis=0, tiled=True)]
    pallas_call x1, Pallas kernels: 3.05 us -> 1.41 us  [merge(): pl.pallas_call(merge_kernel, out_shape=(jax.ShapeDtypeStruct(momentum.sha...]
where the time goes in v2:
time: 115 us
  blocking collectives  104 us (90%)
  Pallas kernels  10.2 us (9%)
    all_to_all x1, blocking collectives, body(): got = lax.all_to_all(start, 'dp', split_axis=0, concat_axis=0, tiled=True)  44.5 us
    all_to_all x1, blocking collectives, body(): lax.all_to_all(update, 'dp', split_axis=0, concat_axis=0, tiled=True)  33.5 us
    all_to_all x1, blocking collectives, polish(): lax.all_to_all(packed, 'mp', split_axis=0, concat_axis=0, tiled=True)  15.2 us
    all_to_all x1, blocking collectives, polish(): lax.all_to_all(copies, 'mp', split_axis=0, concat_axis=0, tiled=True)  10.7 us
    pallas_call x1, Pallas kernels, polish(): pl.pallas_call(lambda *refs: polish_kernel(columns * parts, *refs), out_s...  7.38 us

profile of v2, /device:TPU:1, one launch (start us, length us, event | category | flops | bytes accessed | tf_op | source)
XLA Modules:
  0.0 115.1 jit_solution(15851406277693668450)
XLA Ops:
  0.6 1.4 %shard_map.59 = (f32[32,16,384]{2,1,0:T(8,128)S(1)}, bf16[32,16,384]{2,1,0:T(8,128)(2,1)S(1)}) custom-call(s32[32]{0:T(128)} %old_ref.1, s32[32]{0:T(128)} %new_ref.1, bf16[32,16,384]{2,1,0:T(8,128)(2,1)} %grad_ref.1, f32[32,16,384]{2,1,0:T(8,128)} %mom_ref.1), custom_call_target="tpu_custom_call" | custom-call | tf_op jit(solution)/shard_map/pallas_call | solution.py:42
  2.0 44.5 %all_to_all.20 = bf16[32,16,384]{2,1,0:T(8,128)(2,1)S(1)} all-to-all(bf16[32,16,384]{2,1,0:T(8,128)(2,1)S(1)} %get-tuple-element.6), channel_id=1, replica_groups=mesh['dp'=32,'mp'=16] {'dp'}, dimensions={0} | all-to-all | bytes 786432 | tf_op jit(solution)/shard_map/all_to_all | solution.py:224
  46.6 0.5 shard_map.60
  47.1 15.2 %all_to_all.21 = f16[16,80,128]{2,1,0:T(8,128)(2,1)S(1)} all-to-all(f16[16,80,128]{2,1,0:T(8,128)(2,1)S(1)} %convert_element_type.12), channel_id=1, replica_groups=mesh['dp'=32,'mp'=16] {'mp'}, dimensions={0} | all-to-all | bytes 655360 | tf_op jit(solution)/shard_map/all_to_all | solution.py:199
  62.4 0.2 shard_map.61
  62.7 10.7 %all_to_all.22 = f16[16,80,128]{2,1,0:T(8,128)(2,1)S(1)} all-to-all(f16[16,80,128]{2,1,0:T(8,128)(2,1)S(1)} %broadcast_in_dim.3), channel_id=1, replica_groups=mesh['dp'=32,'mp'=16] {'mp'}, dimensions={0} | all-to-all | bytes 655360 | tf_op jit(solution)/shard_map/all_to_all | solution.py:208
  73.4 7.4 %shard_map.62 = (bf16[512,384]{1,0:T(8,128)(2,1)S(1)}, f32[32,16,384]{2,1,0:T(8,128)}) custom-call(f32[16,80,128]{2,1,0:T(8,128)S(1)} %convert_element_type.15.refs_0_, bf16[512,384]{1,0:T(8,128)(2,1)S(1)} %bitcast.3, f32[32,16,384]{2,1,0:T(8,128)S(1)} %get-tuple-element.7.refs_2_), custom_call_target="tpu_custom_call" | custom-call | tf_op jit(solution)/shard_map/pallas_call | solution.py:209
  80.8 33.5 %all_to_all.23.in_ref = bf16[32,16,384]{2,1,0:T(8,128)(2,1)S(1)} all-to-all(bf16[32,16,384]{2,1,0:T(8,128)(2,1)S(1)} %bitcast.4), channel_id=1, replica_groups=mesh['dp'=32,'mp'=16] {'dp'}, dimensions={0} | all-to-all | bytes 786432 | tf_op jit(solution)/shard_map/all_to_all | solution.py:228
  114.3 0.8 shard_map.63
  (5 shorter events, 0.2 us)

commit v3 on v2

--- a/solution.py
+++ b/solution.py
@@ -219,13 +219,18 @@
     )(copies.astype(f32), start, merged)
 
 
+def exchange(value):
+    order = [device ^ 1 for device in range(value.shape[0])]
+    return lax.all_to_all(value, "dp", split_axis=0, concat_axis=0, tiled=True, axis_index_groups=[order])
+
+
 def body(grad, momentum, old_slot, new_slot):
     merged, start = merge(grad, momentum, old_slot, new_slot)
-    got = lax.all_to_all(start, "dp", split_axis=0, concat_axis=0, tiled=True)
+    got = exchange(start)
     slots, rows, columns = got.shape
     update, merged = polish(got.reshape(slots * rows, columns), merged, lax.axis_size("mp"))
     update = update.reshape(slots, rows, columns)
-    return merged, keep(lax.all_to_all(update, "dp", split_axis=0, concat_axis=0, tiled=True))
+    return merged, keep(exchange(update))
 
 
 def solution(mesh):

time: 115 us -> 113 us (0.983)
  blocking collectives: 104 us -> 102 us
    all_to_all x2, blocking collectives: 78 us -> 76.3 us  [exchange(): lax.all_to_all(value, 'dp', split_axis=0, concat_axis=0, tiled=True, axis...]
where the time goes in v3:
time: 113 us
  blocking collectives  102 us (90%)
  Pallas kernels  10.2 us (9%)
    all_to_all x2, blocking collectives, exchange(): lax.all_to_all(value, 'dp', split_axis=0, concat_axis=0, tiled=True, axis...  76.3 us
    all_to_all x1, blocking collectives, polish(): lax.all_to_all(packed, 'mp', split_axis=0, concat_axis=0, tiled=True)  14.5 us
    all_to_all x1, blocking collectives, polish(): lax.all_to_all(copies, 'mp', split_axis=0, concat_axis=0, tiled=True)  10.8 us
    pallas_call x1, Pallas kernels, polish(): pl.pallas_call(lambda *refs: polish_kernel(columns * parts, *refs), out_s...  7.38 us

profile of v3, /device:TPU:1, one launch (start us, length us, event | category | flops | bytes accessed | tf_op | source)
XLA Modules:
  0.0 112.7 jit_solution(1492659505443343519)
XLA Ops:
  0.6 1.4 %shard_map.59 = (f32[32,16,384]{2,1,0:T(8,128)S(1)}, bf16[32,16,384]{2,1,0:T(8,128)(2,1)S(1)}) custom-call(s32[32]{0:T(128)} %old_ref.1, s32[32]{0:T(128)} %new_ref.1, bf16[32,16,384]{2,1,0:T(8,128)(2,1)} %grad_ref.1, f32[32,16,384]{2,1,0:T(8,128)} %mom_ref.1), custom_call_target="tpu_custom_call" | custom-call | tf_op jit(solution)/shard_map/pallas_call | solution.py:42
  2.0 43.2 %all_to_all.20 = bf16[32,16,384]{2,1,0:T(8,128)(2,1)S(1)} all-to-all(bf16[32,16,384]{2,1,0:T(8,128)(2,1)S(1)} %get-tuple-element.6), channel_id=1, replica_groups={{16,0,48,32,80,64,112,96,144,128,176,160,208,192,240,224,272,256,304,28..., dimensions={0} | all-to-all | bytes 786432 | tf_op jit(solution)/shard_map/all_to_all | solution.py:224
  45.2 0.5 shard_map.60
  45.8 14.5 %all_to_all.21 = f16[16,80,128]{2,1,0:T(8,128)(2,1)S(1)} all-to-all(f16[16,80,128]{2,1,0:T(8,128)(2,1)S(1)} %convert_element_type.12), channel_id=1, replica_groups=mesh['dp'=32,'mp'=16] {'mp'}, dimensions={0} | all-to-all | bytes 655360 | tf_op jit(solution)/shard_map/all_to_all | solution.py:199
  60.3 0.2 shard_map.61
  60.6 10.8 %all_to_all.22 = f16[16,80,128]{2,1,0:T(8,128)(2,1)S(1)} all-to-all(f16[16,80,128]{2,1,0:T(8,128)(2,1)S(1)} %broadcast_in_dim.3), channel_id=1, replica_groups=mesh['dp'=32,'mp'=16] {'mp'}, dimensions={0} | all-to-all | bytes 655360 | tf_op jit(solution)/shard_map/all_to_all | solution.py:208
  71.5 7.4 %shard_map.62 = (bf16[512,384]{1,0:T(8,128)(2,1)S(1)}, f32[32,16,384]{2,1,0:T(8,128)}) custom-call(f32[16,80,128]{2,1,0:T(8,128)S(1)} %convert_element_type.15.refs_0_, bf16[512,384]{1,0:T(8,128)(2,1)S(1)} %bitcast.3, f32[32,16,384]{2,1,0:T(8,128)S(1)} %get-tuple-element.7.refs_2_), custom_call_target="tpu_custom_call" | custom-call | tf_op jit(solution)/shard_map/pallas_call | solution.py:209
  78.9 33.1 %all_to_all.23.in_ref = bf16[32,16,384]{2,1,0:T(8,128)(2,1)S(1)} all-to-all(bf16[32,16,384]{2,1,0:T(8,128)(2,1)S(1)} %bitcast.4), channel_id=1, replica_groups={{16,0,48,32,80,64,112,96,144,128,176,160,208,192,240,224,272,256,304,28..., dimensions={0} | all-to-all | bytes 786432 | tf_op jit(solution)/shard_map/all_to_all | solution.py:224
  112.0 0.8 shard_map.63
  (5 shorter events, 0.2 us)

commit v4 on v3

--- a/solution.py
+++ b/solution.py
@@ -13,8 +13,10 @@
 beta = 0.95
 epsilon = 1e-07
 TILE = 128
+CHUNK = 32
 bf16 = jnp.bfloat16
 f32 = jnp.float32
+f8 = jnp.float8_e4m3fn
 
 
 def merge_kernel(
@@ -102,67 +104,104 @@
     out_ref[...] = jnp.where(marks, power_of, total * power(-power_of))
 
 
-def split(value):
-    high = value.astype(bf16)
-    return high, (value - high.astype(f32)).astype(bf16)
+def put(form, value, row, column, power_of):
+    high_ref, left_ref, right_ref = form
+    size = high_ref.shape[0]
+    columns = slice(column, column + value.shape[1])
+    later = slice(size + column, size + column + value.shape[1])
+    for at in range(0, value.shape[0], CHUNK):
+        chunk = value[at : at + CHUNK]
+        high = chunk.astype(bf16)
+        coarse = (chunk * 2.0**power_of).astype(f8)
+        low = ((chunk - high.astype(f32)) * 2.0 ** (power_of + 8)).astype(f8)
+        lines = slice(row + at, row + at + CHUNK)
+        high_ref[lines, columns] = high
+        left_ref[lines, columns] = coarse
+        left_ref[lines, later] = low
+        right_ref[lines, columns] = low
+        right_ref[slice(size + row + at, size + row + at + CHUNK), columns] = coarse
 
 
 def dot(left, right):
     return jnp.dot(left, right, preferred_element_type=f32)
 
 
-def product(left, right):
-    (lh, ll), (rh, rl) = left, right
-    return dot(jnp.concatenate([lh, ll, lh], axis=1), jnp.concatenate([rh, rh, rl], axis=0))
-
-
-def symmetric(left, right):
-    half = left[0].shape[0] // 2
-    top = product([p[:half] for p in left], right)
-    corner = product([p[half:] for p in left], [p[:, half:] for p in right])
-    return jnp.concatenate([top, jnp.concatenate([top[:, half:].T, corner], axis=1)], axis=0)
-
-
-def polish_kernel(width, packed_ref, x_ref, merged_ref, out_ref, kept_ref, gram_ref, done):
+def product(left, right, rows, columns, power_of):
+    main = dot(left[0][rows, :], right[0][:, columns])
+    return main + dot(left[1][rows, :], right[2][:, columns]) * 2.0 ** -(power_of + 8)
+
+
+def polish_kernel(width, packed_ref, x_ref, merged_ref, out_ref, kept_ref, *scratch):
+    gram_ref, half_ref, rest_ref, pair_ref, done = scratch[:5]
+    gram_form, first_form, half_form, second_form, pair_form = (scratch[at : at + 3] for at in range(5, 20, 3))
     store = pltpu.make_async_copy(merged_ref, kept_ref, done)
     store.start()
-    rows = x_ref.shape[0]
-    parts = packed_ref.shape[0]
+    size = x_ref.shape[0]
+    front, back = slice(0, size // 2), slice(size // 2, size)
+    blocks = ((front, front), (front, back), (back, back))
+
     scale = power(packed_ref[:, 7:8, 0:1])
     row = lax.broadcasted_iota(jnp.int32, (TILE, TILE), 0)
-    below = row > lax.broadcasted_iota(jnp.int32, (TILE, TILE), 1)
-    for at, (r, s) in enumerate(upper(rows // TILE)):
+    column = lax.broadcasted_iota(jnp.int32, (TILE, TILE), 1)
+    total = jnp.zeros((1, 1), f32)
+    for at, (r, s) in enumerate(upper(size // TILE)):
         block = (packed_ref[:, at * 8 : (at + 1) * 8, :] * scale).reshape(TILE, TILE)
         if r == s:
-            block = jnp.where(below, block.T, block)
+            block = jnp.where(row > column, block.T, block)
+            total += jnp.sum(jnp.where(row == column, block, 0.0), keepdims=True)
         gram_ref[r * TILE : (r + 1) * TILE, s * TILE : (s + 1) * TILE] = block
         if r != s:
             gram_ref[s * TILE : (s + 1) * TILE, r * TILE : (r + 1) * TILE] = block.T
-    gram = gram_ref[...]
-    row = lax.broadcasted_iota(jnp.int32, (rows, rows), 0)
-    column = lax.broadcasted_iota(jnp.int32, (rows, rows), 1)
-    diagonal = row == column
-    total = jnp.sum(jnp.where(diagonal, gram, 0.0))
-    inverse = 1.0 / (jnp.sqrt(jnp.full((1, 1), total)) + epsilon)
-    gram = gram * inverse * inverse
-    rests, steps = [], []
-    for step in range(3):
-        g = split(gram)
-        rest = coef_b * gram + coef_c * symmetric(g, g)
-        q = split(rest)
-        rests.append(rest)
-        steps.append(q)
-        if step < 2:
-            half = coef_a * gram + symmetric(g, q)
-        if step == 1:
-            both = coef_a * (rests[0] + rests[1]) + symmetric(q, steps[0])
-            both += jnp.where(diagonal, coef_a * coef_a, 0.0)
-        if step < 2:
-            gram = coef_a * half + symmetric(split(half), q)
-    whole = split(coef_a * both + symmetric(steps[2], split(both)))
+    inverse = 1.0 / (jnp.sqrt(total) + epsilon)
+    for at in range(0, size, CHUNK):
+        chunk = gram_ref[at : at + CHUNK, :] * inverse * inverse
+        gram_ref[at : at + CHUNK, :] = chunk
+        put(gram_form, chunk, at, 0, 7)
+
+    def symmetric(left, right, power_of, finish, form, form_power, kept=None):
+        for rows, columns in blocks:
+            value = finish(product(left, right, rows, columns, power_of), rows, columns)
+            if kept is not None:
+                kept[rows, columns] = value
+            put(form, value, rows.start, columns.start, form_power)
+            if rows != columns:
+                put(form, value.T, columns.start, rows.start, form_power)
+
+    def rest(step):
+        def finish(square, rows, columns):
+            value = coef_b * gram_ref[rows, columns] + coef_c * square
+            if step == 0:
+                rest_ref[rows, columns] = coef_a * value
+            if step == 1:
+                rest_ref[rows, columns] = rest_ref[rows, columns] + coef_a * value
+            return value
+
+        return finish
+
+    def pair(value, rows, columns):
+        value = rest_ref[rows, columns] + value
+        if rows == columns:
+            line = lax.broadcasted_iota(jnp.int32, value.shape, 0)
+            value += jnp.where(line == lax.broadcasted_iota(jnp.int32, value.shape, 1), coef_a**2, 0.0)
+        return value
+
+    once = lambda value, rows, columns: coef_a * gram_ref[rows, columns] + value
+    twice = lambda value, rows, columns: coef_a * half_ref[rows, columns] + value
+    symmetric(gram_form, gram_form, 14, rest(0), first_form, 7)
+    symmetric(gram_form, first_form, 14, once, half_form, 7, half_ref)
+    symmetric(half_form, first_form, 14, twice, gram_form, 7, gram_ref)
+    symmetric(gram_form, gram_form, 14, rest(1), second_form, 7)
+    symmetric(gram_form, second_form, 14, once, half_form, 7, half_ref)
+    symmetric(second_form, first_form, 14, pair, pair_form, 5, pair_ref)
+    symmetric(half_form, second_form, 14, twice, gram_form, 7, gram_ref)
+    symmetric(gram_form, gram_form, 14, rest(2), first_form, 7)
+    near, across, far = (coef_a * pair_ref[r, c] + product(first_form, pair_form, r, c, 12) for r, c in blocks)
     x = x_ref[...]
-    current = dot(whole[0], x) + dot(whole[1], x)
-    out_ref[...] = (0.2 * math.sqrt(width) * inverse * current).astype(bf16)
+    for rows, lines in ((front, (near, across)), (back, (across.T, far))):
+        whole = jnp.concatenate(lines, axis=1)
+        high = whole.astype(bf16)
+        current = dot(high, x) + dot((whole - high.astype(f32)).astype(bf16), x)
+        out_ref[rows] = (0.2 * math.sqrt(width) * inverse * current).astype(bf16)
     store.wait()
 
 
@@ -214,7 +253,9 @@
         ),
         in_specs=[vmem] * 3,
         out_specs=(vmem, pl.BlockSpec(memory_space=pltpu.HBM)),
-        scratch_shapes=[pltpu.VMEM((rows, rows), f32), pltpu.SemaphoreType.DMA],
+        scratch_shapes=[pltpu.VMEM((rows, rows), f32)] * 4
+        + [pltpu.SemaphoreType.DMA]
+        + [pltpu.VMEM((rows, rows), bf16), pltpu.VMEM((rows, 2 * rows), f8), pltpu.VMEM((2 * rows, rows), f8)] * 5,
         compiler_params=params,
     )(copies.astype(f32), start, merged)
 

time: 113 us -> 111 us (0.982)
  Pallas kernels: 10.2 us -> 8.52 us
    pallas_call x1, Pallas kernels: 7.38 us -> 5.69 us  [polish(): pl.pallas_call(lambda *refs: polish_kernel(columns * parts, *refs), out_s...]
where the time goes in v4:
time: 111 us
  blocking collectives  102 us (92%)
  Pallas kernels  8.52 us (8%)
    all_to_all x2, blocking collectives, exchange(): lax.all_to_all(value, 'dp', split_axis=0, concat_axis=0, tiled=True, axis...  76.3 us
    all_to_all x1, blocking collectives, polish(): lax.all_to_all(packed, 'mp', split_axis=0, concat_axis=0, tiled=True)  14.5 us
    all_to_all x1, blocking collectives, polish(): lax.all_to_all(copies, 'mp', split_axis=0, concat_axis=0, tiled=True)  10.8 us
    pallas_call x1, Pallas kernels, polish(): pl.pallas_call(lambda *refs: polish_kernel(columns * parts, *refs), out_s...  5.69 us

profile of v4, /device:TPU:1, one launch (start us, length us, event | category | flops | bytes accessed | tf_op | source)
XLA Modules:
  0.0 111.0 jit_solution(14957444345429111747)
XLA Ops:
  0.6 1.4 %shard_map.59 = (f32[32,16,384]{2,1,0:T(8,128)S(1)}, bf16[32,16,384]{2,1,0:T(8,128)(2,1)S(1)}) custom-call(s32[32]{0:T(128)} %old_ref.1, s32[32]{0:T(128)} %new_ref.1, bf16[32,16,384]{2,1,0:T(8,128)(2,1)} %grad_ref.1, f32[32,16,384]{2,1,0:T(8,128)} %mom_ref.1), custom_call_target="tpu_custom_call" | custom-call | tf_op jit(solution)/shard_map/pallas_call | solution.py:44
  2.0 43.2 %all_to_all.20 = bf16[32,16,384]{2,1,0:T(8,128)(2,1)S(1)} all-to-all(bf16[32,16,384]{2,1,0:T(8,128)(2,1)S(1)} %get-tuple-element.6), channel_id=1, replica_groups={{16,0,48,32,80,64,112,96,144,128,176,160,208,192,240,224,272,256,304,28..., dimensions={0} | all-to-all | bytes 786432 | tf_op jit(solution)/shard_map/all_to_all | solution.py:265
  45.2 0.5 shard_map.60
  45.8 14.5 %all_to_all.21 = f16[16,80,128]{2,1,0:T(8,128)(2,1)S(1)} all-to-all(f16[16,80,128]{2,1,0:T(8,128)(2,1)S(1)} %convert_element_type.12), channel_id=1, replica_groups=mesh['dp'=32,'mp'=16] {'mp'}, dimensions={0} | all-to-all | bytes 655360 | tf_op jit(solution)/shard_map/all_to_all | solution.py:238
  60.3 0.2 shard_map.61
  60.6 10.8 %all_to_all.22 = f16[16,80,128]{2,1,0:T(8,128)(2,1)S(1)} all-to-all(f16[16,80,128]{2,1,0:T(8,128)(2,1)S(1)} %broadcast_in_dim.3), channel_id=1, replica_groups=mesh['dp'=32,'mp'=16] {'mp'}, dimensions={0} | all-to-all | bytes 655360 | tf_op jit(solution)/shard_map/all_to_all | solution.py:247
  71.5 5.7 %shard_map.62 = (bf16[512,384]{1,0:T(8,128)(2,1)S(1)}, f32[32,16,384]{2,1,0:T(8,128)}) custom-call(f32[16,80,128]{2,1,0:T(8,128)S(1)} %convert_element_type.15.refs_0_, bf16[512,384]{1,0:T(8,128)(2,1)S(1)} %bitcast.3, f32[32,16,384]{2,1,0:T(8,128)S(1)} %get-tuple-element.7.refs_2_), custom_call_target="tpu_custom_call" | custom-call | tf_op jit(solution)/shard_map/pallas_call | solution.py:248
  77.2 33.1 %all_to_all.23.in_ref = bf16[32,16,384]{2,1,0:T(8,128)(2,1)S(1)} all-to-all(bf16[32,16,384]{2,1,0:T(8,128)(2,1)S(1)} %bitcast.4), channel_id=1, replica_groups={{16,0,48,32,80,64,112,96,144,128,176,160,208,192,240,224,272,256,304,28..., dimensions={0} | all-to-all | bytes 786432 | tf_op jit(solution)/shard_map/all_to_all | solution.py:265
  110.3 0.8 shard_map.63
  (5 shorter events, 0.2 us)

commit v5 on v4

--- a/solution.py
+++ b/solution.py
@@ -79,29 +79,33 @@
 
 def gram_kernel(x_ref, out_ref):
     x = x_ref[...]
-    gram = lax.dot_general(x, x, (((1,), (1,)), ((), ())), preferred_element_type=f32)
+    half = x.shape[0] // 2
+    split = half // TILE
+    dots = lambda p, q: lax.dot_general(p, q, (((1,), (1,)), ((), ())), preferred_element_type=f32)
+    top, corner = dots(x[:half], x), dots(x[half:], x[half:])
     wide = x.astype(f32)
     bound = jnp.max(jnp.sum(wide * wide, axis=1, keepdims=True), axis=0, keepdims=True)
     power_of = exponent(bound)
-    gram = gram * power(-power_of)
+    scale = power(-power_of)
     parts = out_ref.shape[0]
     for at, (r, s) in enumerate(upper(x.shape[0] // TILE)):
-        block = gram[r * TILE : (r + 1) * TILE, s * TILE : (s + 1) * TILE]
+        gram, r, s = (top, r, s) if r < split else (corner, r - split, s - split)
+        block = gram[r * TILE : (r + 1) * TILE, s * TILE : (s + 1) * TILE] * scale
         if at == 0:
             block = jnp.where(spot(TILE), power_of, block)
         out_ref[:, at * 8 : (at + 1) * 8, :] = block.reshape(parts, 8, TILE)
 
 
 def sum_kernel(parts_ref, out_ref):
+    powers = parts_ref[:, 7:8, 0:1]
+    power_of = jnp.max(powers, axis=0) + math.ceil(math.log2(parts_ref.shape[0]))
+    scales = power(powers - power_of)
     total = jnp.zeros(out_ref.shape, f32)
     for k in range(parts_ref.shape[0]):
-        total += parts_ref[k] * power(parts_ref[k, 7:8, 0:1])
+        total += parts_ref[k] * scales[k]
     row = lax.broadcasted_iota(jnp.int32, out_ref.shape, 0)
     marks = (row == 7) & (lax.broadcasted_iota(jnp.int32, out_ref.shape, 1) == 0)
-    total = jnp.where(marks, 0.0, total)
-    bound = jnp.max(jnp.max(jnp.abs(total), axis=1, keepdims=True), axis=0, keepdims=True)
-    power_of = exponent(bound)
-    out_ref[...] = jnp.where(marks, power_of, total * power(-power_of))
+    out_ref[...] = jnp.where(marks, power_of, total)
 
 
 def put(form, value, row, column, power_of):
@@ -143,20 +147,21 @@
     scale = power(packed_ref[:, 7:8, 0:1])
     row = lax.broadcasted_iota(jnp.int32, (TILE, TILE), 0)
     column = lax.broadcasted_iota(jnp.int32, (TILE, TILE), 1)
-    total = jnp.zeros((1, 1), f32)
-    for at, (r, s) in enumerate(upper(size // TILE)):
-        block = (packed_ref[:, at * 8 : (at + 1) * 8, :] * scale).reshape(TILE, TILE)
+    pieces = [(at, r * TILE, s * TILE) for at, (r, s) in enumerate(upper(size // TILE))]
+    load = lambda at, factor: (packed_ref[:, at * 8 : (at + 1) * 8, :] * factor).reshape(TILE, TILE)
+    diagonal = [jnp.where(row == column, load(at, scale), 0.0) for at, r, s in pieces if r == s]
+    total = jnp.sum(sum(diagonal), keepdims=True)
+    inverse = 1.0 / (jnp.sqrt(total) + epsilon)
+    factor = scale * (inverse * inverse).reshape(1, 1, 1)
+    for at, r, s in pieces:
+        block = load(at, factor)
         if r == s:
             block = jnp.where(row > column, block.T, block)
-            total += jnp.sum(jnp.where(row == column, block, 0.0), keepdims=True)
-        gram_ref[r * TILE : (r + 1) * TILE, s * TILE : (s + 1) * TILE] = block
+        gram_ref[r : r + TILE, s : s + TILE] = block
+        put(gram_form, block, r, s, 7)
         if r != s:
-            gram_ref[s * TILE : (s + 1) * TILE, r * TILE : (r + 1) * TILE] = block.T
-    inverse = 1.0 / (jnp.sqrt(total) + epsilon)
-    for at in range(0, size, CHUNK):
-        chunk = gram_ref[at : at + CHUNK, :] * inverse * inverse
-        gram_ref[at : at + CHUNK, :] = chunk
-        put(gram_form, chunk, at, 0, 7)
+            gram_ref[s : s + TILE, r : r + TILE] = block.T
+            put(gram_form, block.T, s, r, 7)
 
     def symmetric(left, right, power_of, finish, form, form_power, kept=None):
         for rows, columns in blocks:
@@ -197,11 +202,13 @@
     symmetric(gram_form, gram_form, 14, rest(2), first_form, 7)
     near, across, far = (coef_a * pair_ref[r, c] + product(first_form, pair_form, r, c, 12) for r, c in blocks)
     x = x_ref[...]
+    unit = (x.astype(f32) * (inverse * 2.0**8)).astype(f8)
     for rows, lines in ((front, (near, across)), (back, (across.T, far))):
         whole = jnp.concatenate(lines, axis=1)
         high = whole.astype(bf16)
-        current = dot(high, x) + dot((whole - high.astype(f32)).astype(bf16), x)
-        out_ref[rows] = (0.2 * math.sqrt(width) * inverse * current).astype(bf16)
+        low = ((whole - high.astype(f32)) * 2.0**11).astype(f8)
+        current = dot(high, x) * inverse + dot(low, unit) * 2.0**-19
+        out_ref[rows] = (0.2 * math.sqrt(width) * current).astype(bf16)
     store.wait()
 
 

time: 111 us -> 111 us (level)
  no operation moved by 1% of the time
where the time goes in v5:
time: 111 us
  blocking collectives  102 us (92%)
  Pallas kernels  8.26 us (7%)
    all_to_all x2, blocking collectives, exchange(): lax.all_to_all(value, 'dp', split_axis=0, concat_axis=0, tiled=True, axis...  76.3 us
    all_to_all x1, blocking collectives, polish(): lax.all_to_all(packed, 'mp', split_axis=0, concat_axis=0, tiled=True)  14.5 us
    all_to_all x1, blocking collectives, polish(): lax.all_to_all(copies, 'mp', split_axis=0, concat_axis=0, tiled=True)  10.8 us
    pallas_call x1, Pallas kernels, polish(): pl.pallas_call(lambda *refs: polish_kernel(columns * parts, *refs), out_s...  5.6 us

profile of v5, /device:TPU:1, one launch (start us, length us, event | category | flops | bytes accessed | tf_op | source)
XLA Modules:
  0.0 110.8 jit_solution(939697105640114112)
XLA Ops:
  0.6 1.4 %shard_map.59 = (f32[32,16,384]{2,1,0:T(8,128)S(1)}, bf16[32,16,384]{2,1,0:T(8,128)(2,1)S(1)}) custom-call(s32[32]{0:T(128)} %old_ref.1, s32[32]{0:T(128)} %new_ref.1, bf16[32,16,384]{2,1,0:T(8,128)(2,1)} %grad_ref.1, f32[32,16,384]{2,1,0:T(8,128)} %mom_ref.1), custom_call_target="tpu_custom_call" | custom-call | tf_op jit(solution)/shard_map/pallas_call | solution.py:44
  2.0 43.2 %all_to_all.20 = bf16[32,16,384]{2,1,0:T(8,128)(2,1)S(1)} all-to-all(bf16[32,16,384]{2,1,0:T(8,128)(2,1)S(1)} %get-tuple-element.6), channel_id=1, replica_groups={{16,0,48,32,80,64,112,96,144,128,176,160,208,192,240,224,272,256,304,28..., dimensions={0} | all-to-all | bytes 786432 | tf_op jit(solution)/shard_map/all_to_all | solution.py:272
  45.2 0.4 shard_map.60
  45.7 14.5 %all_to_all.21 = f16[16,80,128]{2,1,0:T(8,128)(2,1)S(1)} all-to-all(f16[16,80,128]{2,1,0:T(8,128)(2,1)S(1)} %convert_element_type.12), channel_id=1, replica_groups=mesh['dp'=32,'mp'=16] {'mp'}, dimensions={0} | all-to-all | bytes 655360 | tf_op jit(solution)/shard_map/all_to_all | solution.py:245
  60.3 0.1 shard_map.61
  60.4 10.8 %all_to_all.22 = f16[16,80,128]{2,1,0:T(8,128)(2,1)S(1)} all-to-all(f16[16,80,128]{2,1,0:T(8,128)(2,1)S(1)} %broadcast_in_dim.3), channel_id=1, replica_groups=mesh['dp'=32,'mp'=16] {'mp'}, dimensions={0} | all-to-all | bytes 655360 | tf_op jit(solution)/shard_map/all_to_all | solution.py:254
  71.3 5.6 %shard_map.62 = (bf16[512,384]{1,0:T(8,128)(2,1)S(1)}, f32[32,16,384]{2,1,0:T(8,128)}) custom-call(f32[16,80,128]{2,1,0:T(8,128)S(1)} %convert_element_type.15.refs_0_, bf16[512,384]{1,0:T(8,128)(2,1)S(1)} %bitcast.3, f32[32,16,384]{2,1,0:T(8,128)S(1)} %get-tuple-element.7.refs_2_), custom_call_target="tpu_custom_call" | custom-call | tf_op jit(solution)/shard_map/pallas_call | solution.py:255
  76.9 33.1 %all_to_all.23.in_ref = bf16[32,16,384]{2,1,0:T(8,128)(2,1)S(1)} all-to-all(bf16[32,16,384]{2,1,0:T(8,128)(2,1)S(1)} %bitcast.4), channel_id=1, replica_groups={{16,0,48,32,80,64,112,96,144,128,176,160,208,192,240,224,272,256,304,28..., dimensions={0} | all-to-all | bytes 786432 | tf_op jit(solution)/shard_map/all_to_all | solution.py:272
  110.0 0.8 shard_map.63
  (5 shorter events, 0.2 us)

commit v6 on v3

--- a/solution.py
+++ b/solution.py
@@ -77,29 +77,33 @@
 
 def gram_kernel(x_ref, out_ref):
     x = x_ref[...]
-    gram = lax.dot_general(x, x, (((1,), (1,)), ((), ())), preferred_element_type=f32)
+    half = x.shape[0] // 2
+    split = half // TILE
+    dots = lambda p, q: lax.dot_general(p, q, (((1,), (1,)), ((), ())), preferred_element_type=f32)
+    top, corner = dots(x[:half], x), dots(x[half:], x[half:])
     wide = x.astype(f32)
     bound = jnp.max(jnp.sum(wide * wide, axis=1, keepdims=True), axis=0, keepdims=True)
     power_of = exponent(bound)
-    gram = gram * power(-power_of)
+    scale = power(-power_of)
     parts = out_ref.shape[0]
     for at, (r, s) in enumerate(upper(x.shape[0] // TILE)):
-        block = gram[r * TILE : (r + 1) * TILE, s * TILE : (s + 1) * TILE]
+        gram, r, s = (top, r, s) if r < split else (corner, r - split, s - split)
+        block = gram[r * TILE : (r + 1) * TILE, s * TILE : (s + 1) * TILE] * scale
         if at == 0:
             block = jnp.where(spot(TILE), power_of, block)
         out_ref[:, at * 8 : (at + 1) * 8, :] = block.reshape(parts, 8, TILE)
 
 
 def sum_kernel(parts_ref, out_ref):
+    powers = parts_ref[:, 7:8, 0:1]
+    power_of = jnp.max(powers, axis=0) + math.ceil(math.log2(parts_ref.shape[0]))
+    scales = power(powers - power_of)
     total = jnp.zeros(out_ref.shape, f32)
     for k in range(parts_ref.shape[0]):
-        total += parts_ref[k] * power(parts_ref[k, 7:8, 0:1])
+        total += parts_ref[k] * scales[k]
     row = lax.broadcasted_iota(jnp.int32, out_ref.shape, 0)
     marks = (row == 7) & (lax.broadcasted_iota(jnp.int32, out_ref.shape, 1) == 0)
-    total = jnp.where(marks, 0.0, total)
-    bound = jnp.max(jnp.max(jnp.abs(total), axis=1, keepdims=True), axis=0, keepdims=True)
-    power_of = exponent(bound)
-    out_ref[...] = jnp.where(marks, power_of, total * power(-power_of))
+    out_ref[...] = jnp.where(marks, power_of, total)
 
 
 def split(value):
@@ -130,21 +134,23 @@
     parts = packed_ref.shape[0]
     scale = power(packed_ref[:, 7:8, 0:1])
     row = lax.broadcasted_iota(jnp.int32, (TILE, TILE), 0)
-    below = row > lax.broadcasted_iota(jnp.int32, (TILE, TILE), 1)
-    for at, (r, s) in enumerate(upper(rows // TILE)):
-        block = (packed_ref[:, at * 8 : (at + 1) * 8, :] * scale).reshape(TILE, TILE)
+    column = lax.broadcasted_iota(jnp.int32, (TILE, TILE), 1)
+    pieces = [(at, r * TILE, s * TILE) for at, (r, s) in enumerate(upper(rows // TILE))]
+    load = lambda at, factor: (packed_ref[:, at * 8 : (at + 1) * 8, :] * factor).reshape(TILE, TILE)
+    traces = [jnp.where(row == column, load(at, scale), 0.0) for at, r, s in pieces if r == s]
+    total = jnp.sum(sum(traces), keepdims=True)
+    inverse = 1.0 / (jnp.sqrt(total) + epsilon)
+    factor = scale * (inverse * inverse).reshape(1, 1, 1)
+    for at, r, s in pieces:
+        block = load(at, factor)
         if r == s:
-            block = jnp.where(below, block.T, block)
-        gram_ref[r * TILE : (r + 1) * TILE, s * TILE : (s + 1) * TILE] = block
+            block = jnp.where(row > column, block.T, block)
+        gram_ref[r : r + TILE, s : s + TILE] = block
         if r != s:
-            gram_ref[s * TILE : (s + 1) * TILE, r * TILE : (r + 1) * TILE] = block.T
+            gram_ref[s : s + TILE, r : r + TILE] = block.T
     gram = gram_ref[...]
     row = lax.broadcasted_iota(jnp.int32, (rows, rows), 0)
-    column = lax.broadcasted_iota(jnp.int32, (rows, rows), 1)
-    diagonal = row == column
-    total = jnp.sum(jnp.where(diagonal, gram, 0.0))
-    inverse = 1.0 / (jnp.sqrt(jnp.full((1, 1), total)) + epsilon)
-    gram = gram * inverse * inverse
+    diagonal = row == lax.broadcasted_iota(jnp.int32, (rows, rows), 1)
     rests, steps = [], []
     for step in range(3):
         g = split(gram)

time: 113 us -> 113 us (level)
  no operation moved by 1% of the time
where the time goes in v6:
time: 113 us
  blocking collectives  102 us (90%)
  Pallas kernels  10 us (9%)
    all_to_all x2, blocking collectives, exchange(): lax.all_to_all(value, 'dp', split_axis=0, concat_axis=0, tiled=True, axis...  76.3 us
    all_to_all x1, blocking collectives, polish(): lax.all_to_all(packed, 'mp', split_axis=0, concat_axis=0, tiled=True)  14.5 us
    all_to_all x1, blocking collectives, polish(): lax.all_to_all(copies, 'mp', split_axis=0, concat_axis=0, tiled=True)  10.8 us
    pallas_call x1, Pallas kernels, polish(): pl.pallas_call(lambda *refs: polish_kernel(columns * parts, *refs), out_s...  7.36 us

profile of v6, /device:TPU:1, one launch (start us, length us, event | category | flops | bytes accessed | tf_op | source)
XLA Modules:
  0.0 112.5 jit_solution(10871063903415791194)
XLA Ops:
  0.6 1.4 %shard_map.59 = (f32[32,16,384]{2,1,0:T(8,128)S(1)}, bf16[32,16,384]{2,1,0:T(8,128)(2,1)S(1)}) custom-call(s32[32]{0:T(128)} %old_ref.1, s32[32]{0:T(128)} %new_ref.1, bf16[32,16,384]{2,1,0:T(8,128)(2,1)} %grad_ref.1, f32[32,16,384]{2,1,0:T(8,128)} %mom_ref.1), custom_call_target="tpu_custom_call" | custom-call | tf_op jit(solution)/shard_map/pallas_call | solution.py:42
  2.0 43.2 %all_to_all.20 = bf16[32,16,384]{2,1,0:T(8,128)(2,1)S(1)} all-to-all(bf16[32,16,384]{2,1,0:T(8,128)(2,1)S(1)} %get-tuple-element.6), channel_id=1, replica_groups={{16,0,48,32,80,64,112,96,144,128,176,160,208,192,240,224,272,256,304,28..., dimensions={0} | all-to-all | bytes 786432 | tf_op jit(solution)/shard_map/all_to_all | solution.py:230
  45.2 0.4 shard_map.60
  45.7 14.5 %all_to_all.21 = f16[16,80,128]{2,1,0:T(8,128)(2,1)S(1)} all-to-all(f16[16,80,128]{2,1,0:T(8,128)(2,1)S(1)} %convert_element_type.12), channel_id=1, replica_groups=mesh['dp'=32,'mp'=16] {'mp'}, dimensions={0} | all-to-all | bytes 655360 | tf_op jit(solution)/shard_map/all_to_all | solution.py:205
  60.3 0.1 shard_map.61
  60.4 10.8 %all_to_all.22 = f16[16,80,128]{2,1,0:T(8,128)(2,1)S(1)} all-to-all(f16[16,80,128]{2,1,0:T(8,128)(2,1)S(1)} %broadcast_in_dim.3), channel_id=1, replica_groups=mesh['dp'=32,'mp'=16] {'mp'}, dimensions={0} | all-to-all | bytes 655360 | tf_op jit(solution)/shard_map/all_to_all | solution.py:214
  71.3 7.4 %shard_map.62 = (bf16[512,384]{1,0:T(8,128)(2,1)S(1)}, f32[32,16,384]{2,1,0:T(8,128)}) custom-call(f32[16,80,128]{2,1,0:T(8,128)S(1)} %convert_element_type.15.refs_0_, bf16[512,384]{1,0:T(8,128)(2,1)S(1)} %bitcast.3, f32[32,16,384]{2,1,0:T(8,128)S(1)} %get-tuple-element.7.refs_2_), custom_call_target="tpu_custom_call" | custom-call | tf_op jit(solution)/shard_map/pallas_call | solution.py:215
  78.7 33.1 %all_to_all.23.in_ref = bf16[32,16,384]{2,1,0:T(8,128)(2,1)S(1)} all-to-all(bf16[32,16,384]{2,1,0:T(8,128)(2,1)S(1)} %bitcast.4), channel_id=1, replica_groups={{16,0,48,32,80,64,112,96,144,128,176,160,208,192,240,224,272,256,304,28..., dimensions={0} | all-to-all | bytes 786432 | tf_op jit(solution)/shard_map/all_to_all | solution.py:230
  111.8 0.8 shard_map.63
  (5 shorter events, 0.2 us)

commit v7 on v6

--- a/solution.py
+++ b/solution.py
@@ -189,6 +189,13 @@
     )(value)
 
 
+def share_out(value):
+    side = math.isqrt(value.shape[0])
+    turn = [(at + side // 2) % side for at in range(side)]
+    order = [side * y + x for y in turn for x in turn]
+    return lax.all_to_all(value, "mp", split_axis=0, concat_axis=0, tiled=True, axis_index_groups=[order])
+
+
 def polish(start, merged, parts):
     rows, columns = start.shape
     vmem = pl.BlockSpec(memory_space=pltpu.VMEM)
@@ -202,7 +209,7 @@
         compiler_params=params,
     )(start)
     packed = packed.astype(jnp.float16)
-    packed = lax.all_to_all(packed, "mp", split_axis=0, concat_axis=0, tiled=True)
+    packed = share_out(packed)
     total = pl.pallas_call(
         sum_kernel,
         out_shape=jax.ShapeDtypeStruct(share, f32),
@@ -211,7 +218,7 @@
         compiler_params=params,
     )(packed.astype(f32))
     copies = jnp.broadcast_to(total.astype(jnp.float16), (parts, *share))
-    copies = lax.all_to_all(copies, "mp", split_axis=0, concat_axis=0, tiled=True)
+    copies = share_out(copies)
     return pl.pallas_call(
         lambda *refs: polish_kernel(columns * parts, *refs),
         out_shape=(

time: 113 us -> 110 us (0.973)
  blocking collectives: 102 us -> 98.5 us
    all_to_all x2, blocking collectives: 25.4 us -> 21.9 us  [share_out(): lax.all_to_all(value, 'mp', split_axis=0, concat_axis=0, tiled=True, axis...]
where the time goes in v7:
time: 110 us; the launch traced here: 109 us
  blocking collectives  98.5 us (90%)
  Pallas kernels  10 us (9%)
    all_to_all x2, blocking collectives, exchange(): lax.all_to_all(value, 'dp', split_axis=0, concat_axis=0, tiled=True, axis...  76.6 us
    all_to_all x2, blocking collectives, share_out(): lax.all_to_all(value, 'mp', split_axis=0, concat_axis=0, tiled=True, axis...  21.9 us
    pallas_call x1, Pallas kernels, polish(): pl.pallas_call(lambda *refs: polish_kernel(columns * parts, *refs), out_s...  7.36 us

profile of v7, /device:TPU:1, one launch (start us, length us, event | category | flops | bytes accessed | tf_op | source)
XLA Modules:
  0.0 109.4 jit_solution(10095903434285724465)
XLA Ops:
  0.6 1.4 %shard_map.59 = (f32[32,16,384]{2,1,0:T(8,128)S(1)}, bf16[32,16,384]{2,1,0:T(8,128)(2,1)S(1)}) custom-call(s32[32]{0:T(128)} %old_ref.1, s32[32]{0:T(128)} %new_ref.1, bf16[32,16,384]{2,1,0:T(8,128)(2,1)} %grad_ref.1, f32[32,16,384]{2,1,0:T(8,128)} %mom_ref.1), custom_call_target="tpu_custom_call" | custom-call | tf_op jit(solution)/shard_map/pallas_call | solution.py:42
  2.1 43.2 %all_to_all.20 = bf16[32,16,384]{2,1,0:T(8,128)(2,1)S(1)} all-to-all(bf16[32,16,384]{2,1,0:T(8,128)(2,1)S(1)} %get-tuple-element.6), channel_id=1, replica_groups={{16,0,48,32,80,64,112,96,144,128,176,160,208,192,240,224,272,256,304,28..., dimensions={0} | all-to-all | bytes 786432 | tf_op jit(solution)/shard_map/all_to_all | solution.py:237
  45.2 0.4 shard_map.60
  45.7 11.6 %all_to_all.21 = f16[16,80,128]{2,1,0:T(8,128)(2,1)S(1)} all-to-all(f16[16,80,128]{2,1,0:T(8,128)(2,1)S(1)} %convert_element_type.12), channel_id=1, replica_groups={{10,11,8,9,14,15,12,13,2,3,0,1,6,7,4,5},{26,27,24,25,30,31,28,29,18,19,..., dimensions={0} | all-to-all | bytes 655360 | tf_op jit(solution)/shard_map/all_to_all | solution.py:196
  57.3 0.1 shard_map.61
  57.5 10.3 %all_to_all.22 = f16[16,80,128]{2,1,0:T(8,128)(2,1)S(1)} all-to-all(f16[16,80,128]{2,1,0:T(8,128)(2,1)S(1)} %broadcast_in_dim.3), channel_id=1, replica_groups={{10,11,8,9,14,15,12,13,2,3,0,1,6,7,4,5},{26,27,24,25,30,31,28,29,18,19,..., dimensions={0} | all-to-all | bytes 655360 | tf_op jit(solution)/shard_map/all_to_all | solution.py:196
  67.8 7.4 %shard_map.62 = (bf16[512,384]{1,0:T(8,128)(2,1)S(1)}, f32[32,16,384]{2,1,0:T(8,128)}) custom-call(f32[16,80,128]{2,1,0:T(8,128)S(1)} %convert_element_type.15.refs_0_, bf16[512,384]{1,0:T(8,128)(2,1)S(1)} %bitcast.3, f32[32,16,384]{2,1,0:T(8,128)S(1)} %get-tuple-element.7.refs_2_), custom_call_target="tpu_custom_call" | custom-call | tf_op jit(solution)/shard_map/pallas_call | solution.py:222
  75.2 33.4 %all_to_all.23.in_ref = bf16[32,16,384]{2,1,0:T(8,128)(2,1)S(1)} all-to-all(bf16[32,16,384]{2,1,0:T(8,128)(2,1)S(1)} %bitcast.4), channel_id=1, replica_groups={{16,0,48,32,80,64,112,96,144,128,176,160,208,192,240,224,272,256,304,28..., dimensions={0} | all-to-all | bytes 786432 | tf_op jit(solution)/shard_map/all_to_all | solution.py:237
  108.6 0.8 shard_map.63
  (5 shorter events, 0.2 us)

commit v8 on v7

--- a/solution.py
+++ b/solution.py
@@ -233,7 +233,8 @@
 
 
 def exchange(value):
-    order = [device ^ 1 for device in range(value.shape[0])]
+    count = value.shape[0]
+    order = [(device + count // 2) % count ^ 1 for device in range(count)]
     return lax.all_to_all(value, "dp", split_axis=0, concat_axis=0, tiled=True, axis_index_groups=[order])
 
 

time: 110 us -> 104 us (0.945)
  blocking collectives: 98.5 us -> 92.9 us
    all_to_all x2, blocking collectives: 76.6 us -> 68.6 us  [exchange(): lax.all_to_all(value, 'dp', split_axis=0, concat_axis=0, tiled=True, axis...]
    all_to_all x2, blocking collectives: 21.9 us -> 24.3 us  [share_out(): lax.all_to_all(value, 'mp', split_axis=0, concat_axis=0, tiled=True, axis...]
where the time goes in v8:
time: 104 us
  blocking collectives  92.9 us (89%)
  Pallas kernels  10 us (10%)
    all_to_all x2, blocking collectives, exchange(): lax.all_to_all(value, 'dp', split_axis=0, concat_axis=0, tiled=True, axis...  68.6 us
    all_to_all x2, blocking collectives, share_out(): lax.all_to_all(value, 'mp', split_axis=0, concat_axis=0, tiled=True, axis...  24.3 us
    pallas_call x1, Pallas kernels, polish(): pl.pallas_call(lambda *refs: polish_kernel(columns * parts, *refs), out_s...  7.36 us

profile of v8, /device:TPU:1, one launch (start us, length us, event | category | flops | bytes accessed | tf_op | source)
XLA Modules:
  0.0 103.8 jit_solution(1729069166623880513)
XLA Ops:
  0.6 1.4 %shard_map.59 = (f32[32,16,384]{2,1,0:T(8,128)S(1)}, bf16[32,16,384]{2,1,0:T(8,128)(2,1)S(1)}) custom-call(s32[32]{0:T(128)} %old_ref.1, s32[32]{0:T(128)} %new_ref.1, bf16[32,16,384]{2,1,0:T(8,128)(2,1)} %grad_ref.1, f32[32,16,384]{2,1,0:T(8,128)} %mom_ref.1), custom_call_target="tpu_custom_call" | custom-call | tf_op jit(solution)/shard_map/pallas_call | solution.py:42
  2.1 37.6 %all_to_all.20 = bf16[32,16,384]{2,1,0:T(8,128)(2,1)S(1)} all-to-all(bf16[32,16,384]{2,1,0:T(8,128)(2,1)S(1)} %get-tuple-element.6), channel_id=1, replica_groups={{272,256,304,288,336,320,368,352,400,384,432,416,464,448,496,480,16,0,4..., dimensions={0} | all-to-all | bytes 786432 | tf_op jit(solution)/shard_map/all_to_all | solution.py:238
  39.7 0.4 shard_map.60
  40.1 13.2 %all_to_all.21 = f16[16,80,128]{2,1,0:T(8,128)(2,1)S(1)} all-to-all(f16[16,80,128]{2,1,0:T(8,128)(2,1)S(1)} %convert_element_type.12), channel_id=1, replica_groups={{10,11,8,9,14,15,12,13,2,3,0,1,6,7,4,5},{26,27,24,25,30,31,28,29,18,19,..., dimensions={0} | all-to-all | bytes 655360 | tf_op jit(solution)/shard_map/all_to_all | solution.py:196
  53.4 0.1 shard_map.61
  53.5 11.1 %all_to_all.22 = f16[16,80,128]{2,1,0:T(8,128)(2,1)S(1)} all-to-all(f16[16,80,128]{2,1,0:T(8,128)(2,1)S(1)} %broadcast_in_dim.3), channel_id=1, replica_groups={{10,11,8,9,14,15,12,13,2,3,0,1,6,7,4,5},{26,27,24,25,30,31,28,29,18,19,..., dimensions={0} | all-to-all | bytes 655360 | tf_op jit(solution)/shard_map/all_to_all | solution.py:196
  64.7 7.4 %shard_map.62 = (bf16[512,384]{1,0:T(8,128)(2,1)S(1)}, f32[32,16,384]{2,1,0:T(8,128)}) custom-call(f32[16,80,128]{2,1,0:T(8,128)S(1)} %convert_element_type.15.refs_0_, bf16[512,384]{1,0:T(8,128)(2,1)S(1)} %bitcast.3, f32[32,16,384]{2,1,0:T(8,128)S(1)} %get-tuple-element.7.refs_2_), custom_call_target="tpu_custom_call" | custom-call | tf_op jit(solution)/shard_map/pallas_call | solution.py:222
  72.1 31.0 %all_to_all.23.in_ref = bf16[32,16,384]{2,1,0:T(8,128)(2,1)S(1)} all-to-all(bf16[32,16,384]{2,1,0:T(8,128)(2,1)S(1)} %bitcast.4), channel_id=1, replica_groups={{272,256,304,288,336,320,368,352,400,384,432,416,464,448,496,480,16,0,4..., dimensions={0} | all-to-all | bytes 786432 | tf_op jit(solution)/shard_map/all_to_all | solution.py:238
  103.1 0.8 shard_map.63
  (5 shorter events, 0.2 us)

commit v9 on v7

--- a/solution.py
+++ b/solution.py
@@ -233,7 +233,9 @@
 
 
 def exchange(value):
-    order = [device ^ 1 for device in range(value.shape[0])]
+    chips = value.shape[0] // 2
+    levels = [*range(chips // 2, chips), *reversed(range(chips // 2))]
+    order = [2 * level + core for level in levels for core in (1, 0)]
     return lax.all_to_all(value, "dp", split_axis=0, concat_axis=0, tiled=True, axis_index_groups=[order])
 
 

time: 110 us -> 104 us (0.945)
  blocking collectives: 98.5 us -> 92.6 us
    all_to_all x2, blocking collectives: 76.6 us -> 68.4 us  [exchange(): lax.all_to_all(value, 'dp', split_axis=0, concat_axis=0, tiled=True, axis...]
    all_to_all x2, blocking collectives: 21.9 us -> 24.3 us  [share_out(): lax.all_to_all(value, 'mp', split_axis=0, concat_axis=0, tiled=True, axis...]
where the time goes in v9:
time: 104 us
  blocking collectives  92.6 us (89%)
  Pallas kernels  10 us (10%)
    all_to_all x2, blocking collectives, exchange(): lax.all_to_all(value, 'dp', split_axis=0, concat_axis=0, tiled=True, axis...  68.4 us
    all_to_all x2, blocking collectives, share_out(): lax.all_to_all(value, 'mp', split_axis=0, concat_axis=0, tiled=True, axis...  24.3 us
    pallas_call x1, Pallas kernels, polish(): pl.pallas_call(lambda *refs: polish_kernel(columns * parts, *refs), out_s...  7.36 us

profile of v9, /device:TPU:1, one launch (start us, length us, event | category | flops | bytes accessed | tf_op | source)
XLA Modules:
  0.0 103.5 jit_solution(416925115332208938)
XLA Ops:
  0.6 1.4 %shard_map.59 = (f32[32,16,384]{2,1,0:T(8,128)S(1)}, bf16[32,16,384]{2,1,0:T(8,128)(2,1)S(1)}) custom-call(s32[32]{0:T(128)} %old_ref.1, s32[32]{0:T(128)} %new_ref.1, bf16[32,16,384]{2,1,0:T(8,128)(2,1)} %grad_ref.1, f32[32,16,384]{2,1,0:T(8,128)} %mom_ref.1), custom_call_target="tpu_custom_call" | custom-call | tf_op jit(solution)/shard_map/pallas_call | solution.py:42
  2.0 37.4 %all_to_all.20 = bf16[32,16,384]{2,1,0:T(8,128)(2,1)S(1)} all-to-all(bf16[32,16,384]{2,1,0:T(8,128)(2,1)S(1)} %get-tuple-element.6), channel_id=1, replica_groups={{272,256,304,288,336,320,368,352,400,384,432,416,464,448,496,480,240,22..., dimensions={0} | all-to-all | bytes 786432 | tf_op jit(solution)/shard_map/all_to_all | solution.py:239
  39.4 0.4 shard_map.60
  39.9 13.2 %all_to_all.21 = f16[16,80,128]{2,1,0:T(8,128)(2,1)S(1)} all-to-all(f16[16,80,128]{2,1,0:T(8,128)(2,1)S(1)} %convert_element_type.12), channel_id=1, replica_groups={{10,11,8,9,14,15,12,13,2,3,0,1,6,7,4,5},{26,27,24,25,30,31,28,29,18,19,..., dimensions={0} | all-to-all | bytes 655360 | tf_op jit(solution)/shard_map/all_to_all | solution.py:196
  53.1 0.1 shard_map.61
  53.3 11.1 %all_to_all.22 = f16[16,80,128]{2,1,0:T(8,128)(2,1)S(1)} all-to-all(f16[16,80,128]{2,1,0:T(8,128)(2,1)S(1)} %broadcast_in_dim.3), channel_id=1, replica_groups={{10,11,8,9,14,15,12,13,2,3,0,1,6,7,4,5},{26,27,24,25,30,31,28,29,18,19,..., dimensions={0} | all-to-all | bytes 655360 | tf_op jit(solution)/shard_map/all_to_all | solution.py:196
  64.4 7.4 %shard_map.62 = (bf16[512,384]{1,0:T(8,128)(2,1)S(1)}, f32[32,16,384]{2,1,0:T(8,128)}) custom-call(f32[16,80,128]{2,1,0:T(8,128)S(1)} %convert_element_type.15.refs_0_, bf16[512,384]{1,0:T(8,128)(2,1)S(1)} %bitcast.3, f32[32,16,384]{2,1,0:T(8,128)S(1)} %get-tuple-element.7.refs_2_), custom_call_target="tpu_custom_call" | custom-call | tf_op jit(solution)/shard_map/pallas_call | solution.py:222
  71.8 31.0 %all_to_all.23.in_ref = bf16[32,16,384]{2,1,0:T(8,128)(2,1)S(1)} all-to-all(bf16[32,16,384]{2,1,0:T(8,128)(2,1)S(1)} %bitcast.4), channel_id=1, replica_groups={{272,256,304,288,336,320,368,352,400,384,432,416,464,448,496,480,240,22..., dimensions={0} | all-to-all | bytes 786432 | tf_op jit(solution)/shard_map/all_to_all | solution.py:239
  102.8 0.8 shard_map.63
  (5 shorter events, 0.2 us)

commit v10 on v9

--- a/solution.py
+++ b/solution.py
@@ -234,7 +234,7 @@
 
 def exchange(value):
     chips = value.shape[0] // 2
-    levels = [*range(chips // 2, chips), *reversed(range(chips // 2))]
+    levels = [(level + 11 * chips // 16) % chips for level in range(chips)]
     order = [2 * level + core for level in levels for core in (1, 0)]
     return lax.all_to_all(value, "dp", split_axis=0, concat_axis=0, tiled=True, axis_index_groups=[order])
 

time: 104 us -> 104 us (level)
  no operation moved by 1% of the time
where the time goes in v10:
time: 104 us; the launch traced here: 103 us
  blocking collectives  92.4 us (89%)
  Pallas kernels  10 us (10%)
    all_to_all x2, blocking collectives, exchange(): lax.all_to_all(value, 'dp', split_axis=0, concat_axis=0, tiled=True, axis...  67.4 us
    all_to_all x2, blocking collectives, share_out(): lax.all_to_all(value, 'mp', split_axis=0, concat_axis=0, tiled=True, axis...  25 us
    pallas_call x1, Pallas kernels, polish(): pl.pallas_call(lambda *refs: polish_kernel(columns * parts, *refs), out_s...  7.36 us

profile of v10, /device:TPU:1, one launch (start us, length us, event | category | flops | bytes accessed | tf_op | source)
XLA Modules:
  0.0 103.3 jit_solution(4380378290674131292)
XLA Ops:
  0.6 1.4 %shard_map.59 = (f32[32,16,384]{2,1,0:T(8,128)S(1)}, bf16[32,16,384]{2,1,0:T(8,128)(2,1)S(1)}) custom-call(s32[32]{0:T(128)} %old_ref.1, s32[32]{0:T(128)} %new_ref.1, bf16[32,16,384]{2,1,0:T(8,128)(2,1)} %grad_ref.1, f32[32,16,384]{2,1,0:T(8,128)} %mom_ref.1), custom_call_target="tpu_custom_call" | custom-call | tf_op jit(solution)/shard_map/pallas_call | solution.py:42
  2.0 37.2 %all_to_all.20 = bf16[32,16,384]{2,1,0:T(8,128)(2,1)S(1)} all-to-all(bf16[32,16,384]{2,1,0:T(8,128)(2,1)S(1)} %get-tuple-element.6), channel_id=1, replica_groups={{368,352,400,384,432,416,464,448,496,480,16,0,48,32,80,64,112,96,144,12..., dimensions={0} | all-to-all | bytes 786432 | tf_op jit(solution)/shard_map/all_to_all | solution.py:239
  39.2 0.4 shard_map.60
  39.7 13.3 %all_to_all.21 = f16[16,80,128]{2,1,0:T(8,128)(2,1)S(1)} all-to-all(f16[16,80,128]{2,1,0:T(8,128)(2,1)S(1)} %convert_element_type.12), channel_id=1, replica_groups={{10,11,8,9,14,15,12,13,2,3,0,1,6,7,4,5},{26,27,24,25,30,31,28,29,18,19,..., dimensions={0} | all-to-all | bytes 655360 | tf_op jit(solution)/shard_map/all_to_all | solution.py:196
  53.0 0.1 shard_map.61
  53.2 11.7 %all_to_all.22 = f16[16,80,128]{2,1,0:T(8,128)(2,1)S(1)} all-to-all(f16[16,80,128]{2,1,0:T(8,128)(2,1)S(1)} %broadcast_in_dim.3), channel_id=1, replica_groups={{10,11,8,9,14,15,12,13,2,3,0,1,6,7,4,5},{26,27,24,25,30,31,28,29,18,19,..., dimensions={0} | all-to-all | bytes 655360 | tf_op jit(solution)/shard_map/all_to_all | solution.py:196
  64.9 7.4 %shard_map.62 = (bf16[512,384]{1,0:T(8,128)(2,1)S(1)}, f32[32,16,384]{2,1,0:T(8,128)}) custom-call(f32[16,80,128]{2,1,0:T(8,128)S(1)} %convert_element_type.15.refs_0_, bf16[512,384]{1,0:T(8,128)(2,1)S(1)} %bitcast.3, f32[32,16,384]{2,1,0:T(8,128)S(1)} %get-tuple-element.7.refs_2_), custom_call_target="tpu_custom_call" | custom-call | tf_op jit(solution)/shard_map/pallas_call | solution.py:222
  72.3 30.2 %all_to_all.23.in_ref = bf16[32,16,384]{2,1,0:T(8,128)(2,1)S(1)} all-to-all(bf16[32,16,384]{2,1,0:T(8,128)(2,1)S(1)} %bitcast.4), channel_id=1, replica_groups={{368,352,400,384,432,416,464,448,496,480,16,0,48,32,80,64,112,96,144,12..., dimensions={0} | all-to-all | bytes 786432 | tf_op jit(solution)/shard_map/all_to_all | solution.py:239
  102.5 0.8 shard_map.63
  (5 shorter events, 0.2 us)
